TPU v7x, 512 devices: a whole 4x8x8 slice. The times are simulated.
512 devices in a mesh: cfg: 2 (over core), blk: 32 (over z_lo, y), uly: 8 (over x, z_hi).
Axes of the slice: x: 4, y: 8, z: 8 (z_hi: 2, z_lo: 4; z = z_hi * 4 + z_lo), core: 2. Of those that a mesh axis runs over, the one named last changes fastest.
Arguments:
- hidden: bfloat16 [2, 4608, 3072], P('cfg', ('blk', 'uly')), may hold values from -3 to 3
- qkv: bfloat16 [2, 4608, 3, 3072], P('cfg', ('blk', 'uly')), may hold values from -80 to 80
- step_gate: float32 [2, 28, 3072], P('cfg'), may hold values from -6 to 6
- text_len: int32 [2], P('cfg'), may hold values from 128 to 512, as said below
- step_index: int32 [1], replicated, may hold values from 0 to 27
- guidance: float32 [1], replicated, may hold values from 1.5 to 4.5
- q_gain: float32 [128], replicated, may hold values from 1 to 6
- k_gain: float32 [128], replicated, may hold values from 1 to 6
- out_weight: bfloat16 [3072, 3072], P('uly'), may hold values from -0.109375 to 0.109375
Outputs:
- guided: bfloat16 [4608, 3072], P(('blk', 'uly'), 'cfg')
Inputs may be any that keep to these rules, and one draw needn't show every extreme that they name: `text_len`: in every draw at least one branch has all 512 text tokens valid.
All inputs are finite; a program needn't handle non-finite values.
Results may differ from a plain program's by a relative error of at most 0.02.
The roundings to bfloat16 on the way count: a program that leaves them out, or rounds other values in their place, can miss the bound.
Values may be sent and summed in bfloat16 or wider, within the bound.
A program may use at most 64 MiB of HBM per device.

v0:
```python
import math

import jax
import jax.numpy as jnp
from jax import lax
from jax.sharding import PartitionSpec as P

TXT = 512


epsilon = 1e-06
masked_score = -1e30


def partner(x, axis, distance):
    return lax.ppermute(x, axis, [(i, i ^ 1 << distance) for i in range(lax.axis_size(axis))])


def branch_output(
    hidden_rows, qkv_rows, gate_rows, text_limit, step_index, q_gain, k_gain, out_weight
):
    tok_rows = qkv_rows.shape[0]
    width = qkv_rows.shape[2]
    head_dim = q_gain.shape[0]
    uly_count = lax.axis_size("uly")
    local_width = width // uly_count
    heads_local = local_width // head_dim
    inv_root = 1.0 / math.sqrt(head_dim)
    paired = qkv_rows[:, 0:2].astype(jnp.float32).reshape(tok_rows, 2, width // head_dim, head_dim)
    mean_square = jnp.mean(paired * paired, axis=-1, keepdims=True)
    gains = jnp.stack([q_gain, k_gain])[None, :, None, :]
    normed = (
        (paired * lax.rsqrt(mean_square + epsilon) * gains)
        .astype(jnp.bfloat16)
        .reshape(tok_rows, 2, width)
    )
    packed = jnp.concatenate([normed, qkv_rows[:, 2:3]], axis=1).reshape(
        tok_rows, 3, uly_count, local_width
    )
    moved = lax.all_to_all(packed, "uly", split_axis=2, concat_axis=0, tiled=True)
    queries = moved[:, 0, 0]
    keys_local = moved[:, 1, 0]
    values_local = moved[:, 2, 0]
    query_rows = queries.shape[0]
    query_heads = queries.reshape(query_rows, heads_local, head_dim)

    def attend(state, key_block, value_block, offset):
        running, totals, accum = state
        key_heads = key_block.reshape(-1, heads_local, head_dim)
        value_heads = value_block.reshape(-1, heads_local, head_dim)
        scores = (
            jnp.einsum("qhd,khd->hqk", query_heads, key_heads, preferred_element_type=jnp.float32)
            * inv_root
        )
        positions = offset + jnp.arange(key_heads.shape[0], dtype=jnp.int32)
        kept_keys = (positions >= TXT) | (positions < text_limit)
        scores = jnp.where(kept_keys[None, None, :], scores, masked_score)
        newest = jnp.maximum(running, jnp.max(scores, axis=-1))
        shrink = jnp.exp(running - newest)
        weights = jnp.exp(scores - newest[:, :, None])
        totals = totals * shrink + jnp.sum(weights, axis=-1)
        update = jnp.einsum(
            "hqk,khd->hqd",
            weights.astype(jnp.bfloat16),
            value_heads,
            preferred_element_type=jnp.float32,
        )
        accum = accum * shrink[:, :, None] + update
        return (newest, totals, accum)

    initial = (
        jnp.full((heads_local, query_rows), masked_score, jnp.float32),
        jnp.zeros((heads_local, query_rows), jnp.float32),
        jnp.zeros((heads_local, query_rows, head_dim), jnp.float32),
    )
    key_piece = lax.all_gather(keys_local, "blk", axis=0, tiled=True)
    value_piece = lax.all_gather(values_local, "blk", axis=0, tiled=True)
    key_count = key_piece.shape[0]
    block_count = key_count // query_rows
    key_blocks = key_piece.reshape(block_count, query_rows, local_width)
    value_blocks = value_piece.reshape(block_count, query_rows, local_width)

    def step_block(carried, item):
        key_block, value_block, block_id = item
        return (attend(carried, key_block, value_block, block_id * query_rows), None)

    final_state, unused = lax.scan(
        step_block, initial, (key_blocks, value_blocks, jnp.arange(block_count, dtype=jnp.int32))
    )
    running, totals, accum = final_state
    attn = (
        jnp.transpose(accum / totals[:, :, None], (1, 0, 2))
        .reshape(query_rows, local_width)
        .astype(jnp.bfloat16)
    )
    proj = lax.psum_scatter(
        jnp.dot(attn, out_weight, preferred_element_type=jnp.float32).astype(jnp.bfloat16),
        "uly",
        scatter_dimension=0,
        tiled=True,
    ).astype(jnp.float32)
    gate_row = lax.dynamic_slice_in_dim(gate_rows, step_index[0], 1, 0)
    return (hidden_rows.astype(jnp.float32) + gate_row * proj).astype(jnp.bfloat16)


def on_device(hidden, qkv, step_gate, text_len, step_index, guidance, q_gain, k_gain, out_weight):
    width = qkv.shape[3]
    outputs = branch_output(
        hidden[0], qkv[0], step_gate[0], text_len[0], step_index, q_gain, k_gain, out_weight
    )
    cfg_count = lax.axis_size("cfg")
    half_width = width // cfg_count
    branch_index = lax.axis_index("cfg")
    other = partner(outputs, "cfg", 0)
    is_cond = branch_index == 0
    cond_full = jnp.where(is_cond, outputs, other)
    uncond_full = jnp.where(is_cond, other, outputs)
    cond = lax.dynamic_slice_in_dim(cond_full, branch_index * half_width, half_width, 1).astype(
        jnp.float32
    )
    uncond = lax.dynamic_slice_in_dim(uncond_full, branch_index * half_width, half_width, 1).astype(
        jnp.float32
    )
    return (uncond + guidance[0] * (cond - uncond)).astype(jnp.bfloat16)


def solution(mesh):
    placed = (
        P("cfg", ("blk", "uly"), None),
        P("cfg", ("blk", "uly"), None, None),
        P("cfg", None, None),
        P("cfg"),
        P(),
        P(),
        P(),
        P(),
        P("uly", None),
    )
    return jax.shard_map(
        on_device, mesh=mesh, in_specs=placed, out_specs=P(("blk", "uly"), "cfg"), check_vma=False
    )
```

profile of v0, /device:TPU:1, one launch (start us, length us, event | category | flops | bytes accessed | tf_op | source)
XLA Modules:
  0.0 543.7 jit_solution(9496899438512856751)
XLA Ops:
  6.5 1.3 convert_multiply_fusion.1
  7.9 1.7 slice_reduce_fusion
  10.7 1.3 fusion.11
  12.2 25.2 %all_to_all.18 = bf16[18,3,8,384]{3,0,1,2:T(8,128)(2,1)S(1)} all-to-all(bf16[18,3,8,384]{3,0,1,2:T(8,128)(2,1)S(1)} %copy.31), channel_id=1, replica_groups=mesh['cfg'=2,'blk'=32,'uly'=8] {'uly'}, dimensions={2} | all-to-all | bytes 663552 | tf_op jit(solution)/shard_map/all_to_all | solution.py:40
  37.6 0.7 fusion.19
  39.9 139.0 %all-gather.5.cloned.1.call-done = bf16[4608,1,1,384]{3,0,1,2:T(8,128)(2,1)} async-done(((bf16[144,1,1,384]{3,0,1,2:T(8,128)(2,1)}), bf16[4608,1,1,384]{3,0,1,2:T(8,128)(2,1)}) %all-gather.5.cloned.1.call-update) | async-done | bytes 3538960 | tf_op jit(solution)/shard_map/all_gather | solution.py:76
  178.8 155.0 %all-gather.7.cloned.1.call-done = bf16[4608,1,1,384]{3,0,1,2:T(8,128)(2,1)} async-done(((bf16[144,1,1,384]{3,0,1,2:T(8,128)(2,1)}), bf16[4608,1,1,384]{3,0,1,2:T(8,128)(2,1)}) %all-gather.7.cloned.1.call-update) | async-done | bytes 3538960 | tf_op jit(solution)/shard_map/all_gather | solution.py:77
  333.8 123.9 %while.15 = (s32[]{:T(128)}, f32[3,144]{1,0:T(4,128)S(1)}, f32[3,144]{1,0:T(4,128)S(1)}, f32[3,144,128]{2,1,0:T(8,128)S(1)}, s32[32]{0:T(128)S(1)}, /*index=5*/s...) while((s32[]{:T(128)}, f32[3,144]{1,0:T(4,128)S(1)}, ...), condition=%wide.region_4.5_spmd.clone, body=%wide.region_1.4_spmd.clone.sunk | while | flops 32454580 | bytes 2433477 | solution.py:87
  333.8 1.0 constant_dynamic-slice_fusion.4
  337.7 1.0 constant_dynamic-slice_fusion.4
  341.6 1.0 constant_dynamic-slice_fusion.4
  345.5 1.0 constant_dynamic-slice_fusion.4
  349.3 1.0 constant_dynamic-slice_fusion.4
  353.2 1.0 constant_dynamic-slice_fusion.4
  357.1 1.0 constant_dynamic-slice_fusion.4
  361.0 1.0 constant_dynamic-slice_fusion.4
  364.8 1.0 constant_dynamic-slice_fusion.4
  368.7 1.0 constant_dynamic-slice_fusion.4
  372.6 1.0 constant_dynamic-slice_fusion.4
  376.5 1.0 constant_dynamic-slice_fusion.4
  380.3 1.0 constant_dynamic-slice_fusion.4
  384.2 1.0 constant_dynamic-slice_fusion.4
  388.1 1.0 constant_dynamic-slice_fusion.4
  391.9 1.0 constant_dynamic-slice_fusion.4
  395.8 1.0 constant_dynamic-slice_fusion.4
  399.7 1.0 constant_dynamic-slice_fusion.4
  403.6 1.0 constant_dynamic-slice_fusion.4
  407.4 1.0 constant_dynamic-slice_fusion.4
  411.3 1.0 constant_dynamic-slice_fusion.4
  415.2 1.0 constant_dynamic-slice_fusion.4
  419.1 1.0 constant_dynamic-slice_fusion.4
  422.9 1.0 constant_dynamic-slice_fusion.4
  426.8 1.0 constant_dynamic-slice_fusion.4
  430.7 1.0 constant_dynamic-slice_fusion.4
  434.6 1.0 constant_dynamic-slice_fusion.4
  438.4 1.0 constant_dynamic-slice_fusion.4
  442.3 1.0 constant_dynamic-slice_fusion.4
  446.2 1.0 constant_dynamic-slice_fusion.4
  450.1 1.0 constant_dynamic-slice_fusion.4
  453.9 1.0 constant_dynamic-slice_fusion.4
  458.5 45.6 %fusion = bf16[24,3072]{1,0:T(8,128)(2,1)S(1)} fusion(bf16[144,3072]{1,0:T(8,128)(2,1)S(1)} %convolution_convert_fusion), kind=kCustom, calls=%all-reduce-scatter | all-reduce-scatter fusion | flops 589825 | bytes 1034240
  504.1 1.3 collective-permute-start.1
  505.5 1.3 collective-permute-start.2
  506.8 0.7 constant_dynamic-slice_fusion.2
  507.5 1.3 dynamic-slice.5
  509.4 0.8 concatenate.11
  510.2 1.0 fusion.12
  511.2 24.0 %collective-permute-start = (bf16[18,3072]{1,0:T(8,128)(2,1)S(1)}, bf16[18,3072]{1,0:T(8,128)(2,1)S(1)}, u32[]{:S(2)}, u32[]{:S(2)}) collective-permute-start(bf16[18,3072]{1,0:T(8,128)(2,1)S(1)} %fusion.12), channel_id=1, source_target_pairs={{0,256},{256,0},{1,257},{257,1},{2,258},{258,2},{3,259},{259,3},{4... | collective-permute-start | bytes 331784 | tf_op jit(solution)/shard_map/ppermute | solution.py:16
  (357 shorter events, 72.5 us)
Async XLA Ops:
  6.5 451.3 %copy-start = (bf16[384,3072]{1,0:T(8,128)(2,1)S(1)}, bf16[384,3072]{1,0:T(8,128)(2,1)}, u32[]{:S(2)}) copy-start(bf16[384,3072]{1,0:T(8,128)(2,1)} %param.19) | copy-start | bytes 7077892
  6.5 4.1 copy-start.2
  6.5 4.1 copy-start.1
  6.5 172.3 %all-gather.5.cloned.1.call-start = ((), (), s32[]{:S(2)}) async-start(), calls=%async_computation.1 | async-start | bytes 3649536 | tf_op jit(solution)/shard_map/all_gather | solution.py:76
  38.4 295.5 %all-gather.7.cloned.1.call-start = ((), (), s32[]{:S(2)}) async-start(), calls=%async_computation.2 | async-start | bytes 3649536 | tf_op jit(solution)/shard_map/all_gather | solution.py:77
  504.1 5.3 collective-permute-start.1
  505.5 3.9 collective-permute-start.2
  511.2 25.0 %collective-permute-start = (bf16[18,3072]{1,0:T(8,128)(2,1)S(1)}, bf16[18,3072]{1,0:T(8,128)(2,1)S(1)}, u32[]{:S(2)}, u32[]{:S(2)}) collective-permute-start(bf16[18,3072]{1,0:T(8,128)(2,1)S(1)} %fusion.12), channel_id=1, source_target_pairs={{0,256},{256,0},{1,257},{257,1},{2,258},{258,2},{3,259},{259,3},{4... | collective-permute-start | bytes 331784 | tf_op jit(solution)/shard_map/ppermute | solution.py:16
Sparse Core Ops, SparseCore 0:
  38.5 140.2 all-gather.4
  180.9 152.8 all-gather.6
where the time goes:
time: 546 us; the launch traced here: 544 us
  waiting for transfers between devices  295 us (54%)
  blocking collectives  70.8 us (13%)
  local copies, waits for them, and re-layouts  61.7 us (11%)
  other arithmetic  29 us (5%)
  starting transfers between devices  26.6 us (5%)
  loops' own time  24.2 us (4%)
  matrix products  20.7 us (4%)
  between operations  15.6 us (3%)
    all_gather x1, waiting for transfers between devices, branch_output(): value_piece = lax.all_gather(values_local, 'blk', axis=0, tiled=True)  155 us
    all_gather x1, waiting for transfers between devices, branch_output(): key_piece = lax.all_gather(keys_local, 'blk', axis=0, tiled=True)  139 us
    dynamic_slice x64, local copies, waits for them, and re-layouts, branch_output(): lax.scan(step_block, initial, (key_blocks, value_blocks, jnp.arange(block...  52.7 us
    unnamed x1, blocking collectives  45.6 us
    all_to_all x1, blocking collectives, branch_output(): lax.all_to_all(packed, 'uly', split_axis=2, concat_axis=0, tiled=True)  25.2 us
    another operation x1, loops' own time, branch_output(): lax.scan(step_block, initial, (key_blocks, value_blocks, jnp.arange(block...  24.2 us
    ppermute x1, starting transfers between devices, partner(): lax.ppermute(x, axis, [(i, i ^ 1 << distance) for i in range(lax.axis_siz...  24 us
    or x32, other arithmetic, attend(): kept_keys = (positions >= TXT) | (positions < text_limit)  20.9 us
  transfers between devices with their start and end apart: 5, of which 3 were waited for; matrix products, arithmetic and copies ran while one was open for 0% of the time, Pallas kernels for 0%

commit v1 on v0

v1 whole, which is shorter than its diff:
```python
import functools
import math

import jax
import jax.numpy as jnp
from jax import lax
from jax.experimental import pallas as pl
from jax.experimental.pallas import tpu as pltpu
from jax.sharding import PartitionSpec as P

TXT = 512
HEAD = 128
GROUP = 3
TOK = 18
MAIN = 16
TAIL = TOK - MAIN
PIECE = 4 * MAIN
Z_RUN = 4

epsilon = 1e-06
masked_score = -1e30
MESH = pl.DeviceIdType.MESH
f32, bf16 = jnp.float32, jnp.bfloat16


def kernel(
    sizes,
    hidden_hbm,
    qkv_hbm,
    gate_hbm,
    weight_hbm,
    small_ref,
    out_ref,
    hidden_ref,
    qkv_ref,
    gate_ref,
    weight,
    gate_rows,
    send,
    tail32,
    stage,
    queries,
    kv,
    lifts,
    stat,
    acc,
    part_send,
    part_recv,
    stat_send,
    stat_recv,
    attn,
    attn_other,
    early,
    rows32,
    x_send,
    x_recv,
    z_send,
    z_recv,
    hid_send,
    hid_recv,
    gate_send,
    gate_recv,
    load_sem,
    a2a_send_sem,
    a2a_recv_sem,
    q_send_sem,
    q_recv_sem,
    ring_send_sem,
    ring_recv_sem,
    part_send_sem,
    part_recv_sem,
    cross_send_sem,
    cross_recv_sem,
    x_send_sem,
    x_recv_sem,
    z_send_sem,
    z_recv_sem,
):
    n_u, n_y, n_z = sizes
    block = n_u * TOK
    mains = n_u * MAIN
    tile = n_u * TAIL
    width = n_u * GROUP * HEAD
    half = width // 2
    padded = stat.shape[2]
    chunks, pieces = x_send.shape[0], x_send.shape[2]
    strips = (pieces - 1) // 2
    chunk = strips * HEAD
    n_x = n_u // 2
    far = n_y // 2
    c = lax.axis_index("cfg")
    b = lax.axis_index("blk")
    u = lax.axis_index("uly")
    other = 1 - c
    zl = b // n_y
    y = b % n_y
    mirror = n_z - 1 - zl
    x = u // 2
    zh = u % 2
    across = (c, mirror * n_y + y, u + 1 - 2 * zh)
    right = (c, zl * n_y + (y + 1) % n_y, u)
    left = (c, zl * n_y + (y + n_y - 1) % n_y, u)

    def u_peer(d):
        return (u + d) % n_u

    def u_device(d):
        return (c, b if d % 2 == 0 else mirror * n_y + y, u_peer(d))

    def z_peer(d):
        return (zl + d) % n_z

    def z_device(d):
        return (c, z_peer(d) * n_y + y, u)

    barrier = pltpu.get_barrier_semaphore()
    greet = [u_device(d) for d in range(1, n_u)]
    greet += [z_device(d) for d in range(1, n_z)]
    greet += [right, left, (other, b, u)]
    for who in greet:
        pl.semaphore_signal(barrier, inc=1, device_id=who, device_id_type=MESH)

    loads = [
        pltpu.make_async_copy(src, dst, load_sem.at[i])
        for i, (src, dst) in enumerate(
            [
                (qkv_hbm, qkv_ref),
                (hidden_hbm, hidden_ref),
                (gate_hbm, gate_ref),
                (weight_hbm, weight),
            ]
        )
    ]
    for load in loads:
        load.start()

    def remote(src, dst, send_sem, recv_sem, who):
        return pltpu.make_async_remote_copy(
            src_ref=src,
            dst_ref=dst,
            send_sem=send_sem,
            recv_sem=recv_sem,
            device_id=who,
            device_id_type=MESH,
        )

    started = []

    def go(copy):
        copy.start()
        started.append(copy)

    tail32[...] = jnp.zeros_like(tail32)
    pad = padded - n_z * block
    queries[:, n_z * block : padded, :] = jnp.zeros((GROUP, pad, HEAD), bf16)
    stat[...] = jnp.ones_like(stat)
    loads[0].wait()

    def lay_out(h):
        for g in range(n_u):
            col = (g * GROUP + h) * HEAD
            for part in range(3):
                rows = qkv_ref[:, part, col : col + HEAD].astype(f32)
                if part < 2:
                    gain = small_ref[part : part + 1, :]
                    mean_square = jnp.mean(rows * rows, axis=-1, keepdims=True)
                    rows = rows * lax.rsqrt(mean_square + epsilon) * gain
                send[h, g, MAIN * part : MAIN * (part + 1), :] = rows[:MAIN].astype(bf16)
                tail32[h, g, TAIL * part : TAIL * (part + 1), :] = rows[MAIN:]
        for g in range(n_u):
            send[h, g, 3 * MAIN :, :] = tail32[h, g].astype(bf16)

    def a2a_copy(h, d):
        return remote(
            send.at[h, u_peer(d)],
            stage.at[h, u],
            a2a_send_sem.at[h, d],
            a2a_recv_sem.at[h, n_u - d],
            u_device(d),
        )

    def a2a_wait(h, d):
        remote(
            send.at[h, u_peer(d)],
            stage.at[h, u_peer(d)],
            a2a_send_sem.at[h, d],
            a2a_recv_sem.at[h, d],
            u_device(d),
        ).wait_recv()

    for h in range(GROUP):
        lay_out(h)
        if h == 0:
            pl.semaphore_wait(barrier, len(greet))
        for d in range(1, n_u):
            go(a2a_copy(h, d))
        stage[h, u] = send[h, u]

    def cross_copy(i, src, dst):
        return remote(src, dst, cross_send_sem.at[i], cross_recv_sem.at[i], (other, b, u))

    def half_columns(side):
        return pl.ds(pl.multiple_of(side * half, 128), half)

    loads[1].wait()
    loads[2].wait()
    hid_send[...] = jnp.zeros_like(hid_send)
    hid_send[0:TOK, :] = hidden_ref[:, half_columns(other)]
    step = small_ref[3:4, 0:1]
    gate_rows[...] = functools.reduce(
        jnp.add, [jnp.where(step == float(i), gate_ref[i], 0.0) for i in range(gate_ref.shape[0])]
    )
    gate_send[...] = jnp.broadcast_to(gate_rows[:, half_columns(other)], gate_send.shape)
    hid_copy = cross_copy(GROUP, hid_send, hid_recv)
    gate_copy = cross_copy(GROUP + 1, gate_send, gate_recv)
    go(hid_copy)
    go(gate_copy)

    row = lax.broadcasted_iota(jnp.int32, (block, 1), 0)
    late = row - mains
    source = jnp.where(row < mains, row // MAIN, late // TAIL)
    within = jnp.where(row < mains, row % MAIN, MAIN + late % TAIL)
    source_z = jnp.where(source % 2 == u % 2, zl, mirror)
    token = source_z * (n_y * block) + source * TOK + within
    text_limit = small_ref[2:3, 0:1]
    for slot in range(n_y):
        position = token + slot * block
        kept = (position >= TXT) | (position.astype(f32) < text_limit)
        lifts[slot] = jnp.where(kept, 0.0, masked_score)

    to = lax.broadcasted_iota(jnp.int32, (3 * tile, n_u * MAIN), 0)
    of = lax.broadcasted_iota(jnp.int32, (3 * tile, n_u * MAIN), 1)
    wanted = MAIN * ((to % tile) // TAIL) + TAIL * (to // tile) + to % TAIL
    pick = jnp.where(of == wanted, 1.0, 0.0).astype(bf16)

    def query_rows(h, z):
        return queries.at[h, pl.ds(pl.multiple_of(block * z, MAIN), block), :]

    def assemble(h):
        for d in range(1, n_u):
            a2a_wait(h, d)
        tails = stage[h, :, 3 * MAIN :, :].reshape(n_u * MAIN, HEAD)
        fixed = jnp.dot(pick, tails, preferred_element_type=f32).astype(bf16)
        for part in range(2):
            rows = stage[h, :, MAIN * (part + 1) : MAIN * (part + 2), :]
            kv[y, h, part, :mains, :] = rows.reshape(mains, HEAD)
            kv[y, h, part, mains:, :] = fixed[tile * (part + 1) : tile * (part + 2)]
        ring_step(h, 1)
        main_rows = pl.ds(pl.multiple_of(block * zl, MAIN), mains)
        tail_rows = pl.ds(pl.multiple_of(block * zl + mains, MAIN), tile)
        queries[h, main_rows, :] = stage[h, :, 0:MAIN, :].reshape(mains, HEAD)
        queries[h, tail_rows, :] = fixed[:tile]
        for d in range(1, n_z):
            go(
                remote(
                    query_rows(h, zl),
                    query_rows(h, zl),
                    q_send_sem.at[h, d],
                    q_recv_sem.at[h, n_z - d],
                    z_device(d),
                )
            )

    def await_queries(h):
        for d in range(1, n_z):
            rows = query_rows(h, z_peer(d))
            remote(rows, rows, q_send_sem.at[h, d], q_recv_sem.at[h, d], z_device(d)).wait_recv()

    def behind(s):
        return (y - s + n_y) % n_y

    def ahead(s):
        return (y + s) % n_y

    def ring_piece(h, s, way, slot):
        piece = kv.at[slot, h] if s < far else kv.at[slot, h, way]
        return remote(
            piece,
            piece,
            ring_send_sem.at[h, s, way],
            ring_recv_sem.at[h, s, way],
            right if way == 0 else left,
        )

    def ring_wait(h, s):
        for way in range(2):
            ring_piece(h, s, way, behind(s) if way == 0 else ahead(s)).wait_recv()

    def ring_step(h, s):
        for way in range(2):
            if s > 1:
                slot = behind(s - 1) if way == 0 else ahead(s - 1)
                ring_piece(h, s - 1, way, slot).wait_recv()
            go(ring_piece(h, s, way, behind(s - 1) if way == 0 else ahead(s - 1)))

    factor = math.log2(math.e) / math.sqrt(HEAD)
    rows_rows = (((1,), (1,)), ((), ()))
    first_first = (((0,), (0,)), ((), ()))

    def attend(h, slots, first=False):
        keys = jnp.concatenate([kv[slot, h, 0] for slot in slots], axis=0)
        values = jnp.concatenate([kv[slot, h, 1] for slot in slots], axis=0)
        lift = jnp.concatenate([lifts[slot] for slot in slots], axis=0)
        scores = (
            lax.dot_general(keys, queries[h], rows_rows, preferred_element_type=f32) + lift
        )
        top = jnp.max(scores, axis=0, keepdims=True)
        if not first:
            before = stat[h, 0:1, :]
            top = jnp.maximum(top, before)
            shrink = jnp.exp2((before - top) * factor)
        weights = jnp.exp2((scores - top) * factor)
        summed = jnp.sum(weights, axis=0, keepdims=True)
        mixed = lax.dot_general(
            values, weights.astype(bf16), first_first, preferred_element_type=f32
        )
        stat[h, 0:1, :] = top
        if first:
            stat[h, 1:2, :] = summed
            acc[h] = mixed
        else:
            stat[h, 1:2, :] = stat[h, 1:2, :] * shrink + summed
            acc[h] = acc[h] * shrink + mixed

    def part_copies(h, d, i, z, mine, theirs):
        return [
            remote(
                stat_send.at[h, z],
                stat_recv.at[h, i],
                part_send_sem.at[h, 0, d],
                part_recv_sem.at[h, 0, theirs],
                z_device(d),
            ),
            remote(
                part_send.at[h, z],
                part_recv.at[h, i],
                part_send_sem.at[h, 1, d],
                part_recv_sem.at[h, 1, theirs],
                z_device(d),
            ),
        ]

    def hand_back(h):
        stats = stat[h]
        for i in range(n_z):
            moved = stats if i == 0 else pltpu.roll(stats, padded - block * i, 1)
            stat_send[h, i] = jnp.concatenate([moved[0:4, :128], moved[0:4, 128:256]], axis=0)
        turned = jnp.transpose(acc[h]).astype(bf16)
        for i in range(n_z):
            part_send[h, i] = turned[block * i : block * (i + 1)]
        for d in range(1, n_z):
            for copy in part_copies(h, d, n_z - d - 1, z_peer(d), d, n_z - d):
                go(copy)

    def combine(h):
        for d in range(1, n_z):
            for copy in part_copies(h, d, d - 1, z_peer(d), d, d):
                copy.wait_recv()
        held = [stat_send[h, zl]] + [stat_recv[h, d] for d in range(n_z - 1)]
        top = functools.reduce(jnp.maximum, held)
        shares = [jnp.exp2((s - top) * factor) for s in held]
        lines = []
        for at in (0, 4):
            whole = sum(w[at : at + 1] * s[at + 1 : at + 2] for w, s in zip(shares, held))
            lines += [w[at : at + 1] / whole for w in shares]
        columns = jnp.transpose(jnp.concatenate(lines, axis=0))
        terms = [part_send[h, zl]] + [part_recv[h, d] for d in range(n_z - 1)]
        early_rows = sum(t[:128].astype(f32) * columns[:, k : k + 1] for k, t in enumerate(terms))
        late_rows = sum(
            t[128:].astype(f32) * columns[: block - 128, n_z + k : n_z + k + 1]
            for k, t in enumerate(terms)
        )
        attn[h, :128, :] = early_rows.astype(bf16)
        attn[h, 128:, :] = late_rows.astype(bf16)
        copy = cross_copy(h, attn.at[h], attn_other.at[h])
        go(copy)
        return copy

    assemble(0)
    assemble(1)
    ring_step(0, 2)
    await_queries(0)
    attend(0, [y, behind(1), ahead(1)], first=True)
    assemble(2)
    ring_step(0, 3)
    ring_step(1, 2)
    attend(0, [behind(2), ahead(2)])
    await_queries(1)
    attend(1, [y, behind(1), ahead(1)], first=True)
    ring_step(0, 4)
    ring_step(1, 3)
    ring_step(2, 2)
    attend(1, [behind(2), ahead(2)])
    await_queries(2)
    attend(2, [y, behind(1), ahead(1)], first=True)
    ring_wait(0, far)
    attend(0, [behind(3), ahead(3), ahead(far)])
    hand_back(0)
    ring_step(1, 4)
    ring_step(2, 3)
    attend(2, [behind(2), ahead(2)])
    ring_wait(1, far)
    attend(1, [behind(3), ahead(3), ahead(far)])
    hand_back(1)
    ring_step(2, 4)
    attend(2, [behind(3), ahead(3)])
    ring_wait(2, far)
    attend(2, [ahead(far)])
    settled = len(started)
    hand_back(2)

    guide = small_ref[4:5, 0:1]
    coefficient = jnp.where(c == 0, guide, 1.0 - guide)
    crossed = [combine(h) for h in range(GROUP - 1)]
    loads[3].wait()
    gate_copy.wait_recv()
    for copy in crossed:
        copy.wait_recv()
    done = HEAD * (GROUP - 1)

    def project(n, rows, own, others):
        at = pl.ds(pl.multiple_of(c * half + chunk * n, 128), chunk)
        cols = slice(chunk * n, chunk * (n + 1))
        scale = gate_rows[:, at] * coefficient
        scale_other = gate_recv[0:1, cols] * (1.0 - coefficient)
        part = weight[rows, at]
        return (
            jnp.dot(own, part, preferred_element_type=f32) * scale
            + jnp.dot(others, part, preferred_element_type=f32) * scale_other
        )

    first_own = jnp.concatenate([attn[h] for h in range(GROUP - 1)], axis=1)
    first_other = jnp.concatenate([attn_other[h] for h in range(GROUP - 1)], axis=1)
    for n in range(chunks):
        early[n] = project(n, slice(0, done), first_own, first_other)
    hid_copy.wait_recv()
    kept_hidden = hidden_ref[:, half_columns(c)].astype(f32)
    residual = kept_hidden * coefficient + hid_recv[0:TOK, :].astype(f32) * (1.0 - coefficient)
    for copy in started[:settled]:
        copy.wait_send()
    combine(GROUP - 1).wait_recv()

    def x_copy(n, d, i, theirs):
        there = (x + d) % n_x
        return remote(
            x_send.at[n, there],
            x_recv.at[n, i],
            x_send_sem.at[n, d],
            x_recv_sem.at[n, theirs],
            (c, b, 2 * there + zh),
        )

    def z_copy(n):
        return remote(z_send.at[n], z_recv.at[n], z_send_sem.at[n], z_recv_sem.at[n], across)

    last_own, last_other = attn[GROUP - 1], attn_other[GROUP - 1]
    for n in range(chunks):
        summed = early[n] + project(n, slice(done, done + HEAD), last_own, last_other)
        for i in range(strips):
            strip = summed[:, HEAD * i : HEAD * (i + 1)]
            for j in range(n_u):
                rows32[n, j // 2, (j % 2) * strips + i] = strip[MAIN * j : MAIN * (j + 1)]
            for j in range(n_x):
                rows32[n, j, 2 * strips, 2 * TAIL * i : 2 * TAIL * (i + 1), :] = strip[
                    mains + 2 * TAIL * j : mains + 2 * TAIL * (j + 1)
                ]
        x_send[n] = rows32[n].astype(bf16)
        for d in range(1, n_x):
            go(x_copy(n, d, n_x - d - 1, n_x - d))

    sums = []
    for n in range(chunks):
        for d in range(1, n_x):
            x_copy(n, d, d - 1, d).wait_recv()
        summed = rows32[n, x]
        for d in range(1, n_x):
            summed += x_recv[n, d - 1].astype(f32)
        is_low = zh == 0
        here = jnp.where(is_low, summed[:strips], summed[strips : 2 * strips])
        there = jnp.where(is_low, summed[strips : 2 * strips], summed[:strips])
        z_send[n, :strips] = there.astype(bf16)
        z_send[n, strips] = summed[2 * strips].astype(bf16)
        go(z_copy(n))
        sums.append((here, summed[2 * strips]))
    for n in range(chunks):
        z_copy(n).wait_recv()
        here, tail = sums[n]
        tail = tail + z_recv[n, strips].astype(f32)
        for i in range(strips):
            cols = slice(chunk * n + HEAD * i, chunk * n + HEAD * (i + 1))
            main_rows = here[i] + z_recv[n, i].astype(f32)
            at = 2 * TAIL * i
            tail_rows = jnp.where(is_low, tail[at : at + TAIL], tail[at + TAIL : at + 2 * TAIL])
            out_ref[0:MAIN, cols] = (residual[0:MAIN, cols] + main_rows).astype(bf16)
            out_ref[MAIN:TOK, cols] = (residual[MAIN:TOK, cols] + tail_rows).astype(bf16)
    for copy in started[settled:]:
        copy.wait_send()


def on_device(sizes, hidden, qkv, step_gate, text_len, step_index, guidance, q_gain, k_gain, out_weight):
    n_u, n_y, n_z = sizes
    block = n_u * TOK
    width = n_u * GROUP * HEAD
    half = width // 2
    chunks = 3
    chunk = half // chunks
    strips = chunk // HEAD
    pieces = 2 * strips + 1
    n_x = n_u // 2
    padded = -(-n_z * block // 128) * 128
    far = n_y // 2
    steps = step_gate.shape[1]
    vmem, dma = pltpu.VMEM, pltpu.SemaphoreType.DMA
    in_hbm = pl.BlockSpec(memory_space=pltpu.HBM)
    row = lax.broadcasted_iota(jnp.int32, (8, HEAD), 0)
    small = jnp.where(row == 0, q_gain[None, :], k_gain[None, :])
    for at, scalar in ((2, text_len), (3, step_index), (4, guidance)):
        small = jnp.where(row == at, scalar.astype(f32), small)
    return pl.pallas_call(
        functools.partial(kernel, sizes),
        out_shape=jax.ShapeDtypeStruct((TOK, half), bf16),
        in_specs=[in_hbm] * 4 + [pl.BlockSpec(memory_space=vmem)],
        out_specs=pl.BlockSpec(memory_space=vmem),
        scratch_shapes=[
            vmem((TOK, width), bf16),
            vmem((TOK, 3, width), bf16),
            vmem((steps, 1, width), f32),
            vmem((GROUP * HEAD, width), bf16),
            vmem((1, width), f32),
            vmem((GROUP, n_u, PIECE, HEAD), bf16),
            vmem((GROUP, n_u, MAIN, HEAD), f32),
            vmem((GROUP, n_u, PIECE, HEAD), bf16),
            vmem((GROUP, padded, HEAD), bf16),
            vmem((n_y, GROUP, 2, block, HEAD), bf16),
            vmem((n_y, block, 1), f32),
            vmem((GROUP, 8, padded), f32),
            vmem((GROUP, HEAD, padded), f32),
            vmem((GROUP, n_z, block, HEAD), bf16),
            vmem((GROUP, n_z - 1, block, HEAD), bf16),
            vmem((GROUP, n_z, 8, 128), f32),
            vmem((GROUP, n_z - 1, 8, 128), f32),
            vmem((GROUP, block, HEAD), bf16),
            vmem((GROUP, block, HEAD), bf16),
            vmem((chunks, block, chunk), f32),
            vmem((chunks, n_x, pieces, MAIN, HEAD), f32),
            vmem((chunks, n_x, pieces, MAIN, HEAD), bf16),
            vmem((chunks, n_x - 1, pieces, MAIN, HEAD), bf16),
            vmem((chunks, strips + 1, MAIN, HEAD), bf16),
            vmem((chunks, strips + 1, MAIN, HEAD), bf16),
            vmem((32, half), bf16),
            vmem((32, half), bf16),
            vmem((8, half), f32),
            vmem((8, half), f32),
            dma((4,)),
            dma((GROUP, n_u)),
            dma((GROUP, n_u)),
            dma((GROUP, n_z)),
            dma((GROUP, n_z)),
            dma((GROUP, far + 1, 2)),
            dma((GROUP, far + 1, 2)),
            dma((GROUP, 2, n_z)),
            dma((GROUP, 2, n_z)),
            dma((GROUP + 2,)),
            dma((GROUP + 2,)),
            dma((chunks, n_x)),
            dma((chunks, n_x)),
            dma((chunks,)),
            dma((chunks,)),
        ],
        compiler_params=pltpu.CompilerParams(
            collective_id=0, has_side_effects=True, vmem_limit_bytes=55104 * 1024
        ),
        cost_estimate=pl.CostEstimate(
            flops=2 * n_z * n_y * block * block * GROUP * HEAD * 2,
            bytes_accessed=8 * 1024 * 1024,
            transcendentals=n_z * n_y * block * block * GROUP,
        ),
    )(
        hidden[0],
        qkv[0],
        jnp.transpose(step_gate, (1, 0, 2)),
        out_weight,
        small,
    )


def solution(mesh):
    placed = (
        P("cfg", ("blk", "uly"), None),
        P("cfg", ("blk", "uly"), None, None),
        P("cfg", None, None),
        P("cfg"),
        P(),
        P(),
        P(),
        P(),
        P("uly", None),
    )
    sizes = (mesh.shape["uly"], mesh.shape["blk"] // Z_RUN, Z_RUN)
    return jax.shard_map(
        functools.partial(on_device, sizes),
        mesh=mesh,
        in_specs=placed,
        out_specs=P(("blk", "uly"), "cfg"),
        check_vma=False,
    )
```

time: 546 us -> 70.1 us (0.13)
  waiting for transfers between devices: 295 us -> 0 us
  blocking collectives: 70.8 us -> 0 us
  Pallas kernels: 0 us -> 66.4 us
  local copies, waits for them, and re-layouts: 61.7 us -> 0.64 us
  other arithmetic: 29 us -> 0.76 us
  starting transfers between devices: 26.6 us -> 0 us
  loops' own time: 24.2 us -> 0 us
  matrix products: 20.7 us -> 0 us
  between operations: 15.6 us -> 1.96 us
    all_gather x2 -> x0, waiting for transfers between devices: 294 us -> none  [the longest x1 155 us: branch_output(): value_piece = lax.all_gather(values_local, 'blk', axis=0, tiled=True)]
    pallas_call x0 -> x1, Pallas kernels: none -> 66.4 us  [on_device(): pl.pallas_call(functools.partial(kernel, sizes), out_shape=jax.ShapeDtype...]
    dynamic_slice x65 -> x0, local copies, waits for them, and re-layouts: 53.5 us -> none  [the longest x64 52.7 us: branch_output(): lax.scan(step_block, initial, (key_blocks, value_blocks, jnp.arange(block...]
    unnamed x1 -> x0, blocking collectives: 45.6 us -> none
    all_to_all x1 -> x0, blocking collectives: 25.2 us -> none  [branch_output(): lax.all_to_all(packed, 'uly', split_axis=2, concat_axis=0, tiled=True)]
    another operation x1 -> x0, loops' own time: 24.2 us -> none  [branch_output(): lax.scan(step_block, initial, (key_blocks, value_blocks, jnp.arange(block...]
    ppermute x1 -> x0, starting transfers between devices: 24 us -> none  [partner(): lax.ppermute(x, axis, [(i, i ^ 1 << distance) for i in range(lax.axis_siz...]
    or x32 -> x0, other arithmetic: 20.9 us -> none  [attend(): kept_keys = (positions >= TXT) | (positions < text_limit)]
  transfers between devices with their start and end apart: 5 -> 0, of which waited for: 3 -> 0; matrix products, arithmetic and copies ran while one was open for 0% -> 0% of each run, Pallas kernels for 0% -> 0%
where the time goes in v1:
time: 70.1 us; the launch traced here: 69.8 us
  Pallas kernels  66.4 us (95%)
  between operations  1.96 us (3%)
  other arithmetic  0.76 us (1%)
    pallas_call x1, Pallas kernels, on_device(): pl.pallas_call(functools.partial(kernel, sizes), out_shape=jax.ShapeDtype...  66.4 us

profile of v1, /device:TPU:1, one launch (start us, length us, event | category | flops | bytes accessed | tf_op | source)
XLA Modules:
  0.0 69.8 jit_solution(3847614088603452004)
XLA Ops:
  2.0 0.8 %select_select_fusion.small_ref = f32[8,128]{1,0:T(8,128)S(1)} fusion(f32[128]{0:T(128)} %param.16, f32[128]{0:T(128)} %param.15, f32[]{:T(128)} %bitcast.5, f32[]{:T(128)} %bitcast.4, f32[]{:T(128)} %bitcast.6, pred[8]{0:T(512)(128)(4,1)S(1)} %get-tuple-element.5, pred[8]{0:T(512)(128)(4,1)S(1)} %get-tuple-element.6, pred[8]{0:T(512)(128)(4,1)S(1)} %get-tuple-element.7, ...), kind=kLoop, calls=%fused_computation | loop fusion | flops 4096 | bytes 5164 | tf_op jit(solution)/shard_map/jit(_where)/select_n | solution.py:518
  2.7 66.4 %shard_map.94 = bf16[18,1536]{1,0:T(8,128)(2,1)S(1)} custom-call(bf16[18,3072]{1,0:T(8,128)(2,1)} %bitcast.9, bf16[18,3,3072]{2,1,0:T(4,128)(2,1)} %bitcast.7, f32[28,1,3072]{2,1,0:T(1,128)} %bitcast.8, bf16[384,3072]{1,0:T(8,128)(2,1)} %weight_hbm.1, f32[8,128]{1,0:T(8,128)S(1)} %select_select_fusion.small_ref), custom_call_target="tpu_custom_call" | custom-call | flops 1019215872 | bytes 8388608 | tf_op jit(solution)/shard_map/pallas_call | solution.py:519
  69.1 0.6 copy.14
  (2 shorter events, 0.0 us)

commit v2 on v1

--- a/solution.py
+++ b/solution.py
@@ -100,6 +100,8 @@
     across = (c, mirror * n_y + y, u + 1 - 2 * zh)
     right = (c, zl * n_y + (y + 1) % n_y, u)
     left = (c, zl * n_y + (y + n_y - 1) % n_y, u)
+    right_two = (c, zl * n_y + (y + 2) % n_y, u)
+    left_two = (c, zl * n_y + (y + n_y - 2) % n_y, u)
 
     def u_peer(d):
         return (u + d) % n_u
@@ -116,6 +118,7 @@
     barrier = pltpu.get_barrier_semaphore()
     greet = [u_device(d) for d in range(1, n_u)]
     greet += [z_device(d) for d in range(1, n_z)]
+    greet += [right_two, left_two]
     greet += [right, left, (other, b, u)]
     for who in greet:
         pl.semaphore_signal(barrier, inc=1, device_id=who, device_id_type=MESH)
@@ -282,6 +285,19 @@
             right if way == 0 else left,
         )
 
+    def ring_leap(h):
+        for way in range(2):
+            piece = kv.at[behind(far - 2) if way == 0 else ahead(far - 2), h, way]
+            go(
+                remote(
+                    piece,
+                    piece,
+                    ring_send_sem.at[h, far, way],
+                    ring_recv_sem.at[h, far, way],
+                    right_two if way == 0 else left_two,
+                )
+            )
+
     def ring_wait(h, s):
         for way in range(2):
             ring_piece(h, s, way, behind(s) if way == 0 else ahead(s)).wait_recv()
@@ -394,18 +410,18 @@
     await_queries(2)
     attend(2, [y, behind(1), ahead(1)], first=True)
     ring_wait(0, far)
+    ring_step(1, 4)
+    ring_step(2, 3)
+    ring_leap(2)
     attend(0, [behind(3), ahead(3), ahead(far)])
     hand_back(0)
-    ring_step(1, 4)
-    ring_step(2, 3)
     attend(2, [behind(2), ahead(2)])
     ring_wait(1, far)
     attend(1, [behind(3), ahead(3), ahead(far)])
     hand_back(1)
-    ring_step(2, 4)
-    attend(2, [behind(3), ahead(3)])
+    ring_wait(2, 3)
     ring_wait(2, far)
-    attend(2, [ahead(far)])
+    attend(2, [behind(3), ahead(3), ahead(far)])
     settled = len(started)
     hand_back(2)
 

time: 70.1 us -> 69.2 us (0.987)
  no operation moved by 1% of the time
where the time goes in v2:
time: 69.2 us; the launch traced here: 69.1 us
  Pallas kernels  65.7 us (95%)
  between operations  1.96 us (3%)
  other arithmetic  0.76 us (1%)
    pallas_call x1, Pallas kernels, on_device(): pl.pallas_call(functools.partial(kernel, sizes), out_shape=jax.ShapeDtype...  65.7 us

profile of v2, /device:TPU:1, one launch (start us, length us, event | category | flops | bytes accessed | tf_op | source)
XLA Modules:
  0.0 69.1 jit_solution(352129496704651485)
XLA Ops:
  2.0 0.8 %select_select_fusion.small_ref = f32[8,128]{1,0:T(8,128)S(1)} fusion(f32[128]{0:T(128)} %param.16, f32[128]{0:T(128)} %param.15, f32[]{:T(128)} %bitcast.5, f32[]{:T(128)} %bitcast.4, f32[]{:T(128)} %bitcast.6, pred[8]{0:T(512)(128)(4,1)S(1)} %get-tuple-element.5, pred[8]{0:T(512)(128)(4,1)S(1)} %get-tuple-element.6, pred[8]{0:T(512)(128)(4,1)S(1)} %get-tuple-element.7, ...), kind=kLoop, calls=%fused_computation | loop fusion | flops 4096 | bytes 5164 | tf_op jit(solution)/shard_map/jit(_where)/select_n | solution.py:534
  2.7 65.7 %shard_map.94 = bf16[18,1536]{1,0:T(8,128)(2,1)S(1)} custom-call(bf16[18,3072]{1,0:T(8,128)(2,1)} %bitcast.9, bf16[18,3,3072]{2,1,0:T(4,128)(2,1)} %bitcast.7, f32[28,1,3072]{2,1,0:T(1,128)} %bitcast.8, bf16[384,3072]{1,0:T(8,128)(2,1)} %weight_hbm.1, f32[8,128]{1,0:T(8,128)S(1)} %select_select_fusion.small_ref), custom_call_target="tpu_custom_call" | custom-call | flops 1019215872 | bytes 8388608 | tf_op jit(solution)/shard_map/pallas_call | solution.py:535
  68.4 0.6 copy.14
  (2 shorter events, 0.0 us)
